TPU v7x, 512 devices: a whole 4x8x8 slice. The times are simulated.
512 devices in a mesh: row: 16 (over x, y_hi, core), col: 32 (over y_lo, z).
Axes of the slice: x: 4, y: 8 (y_hi: 2, y_lo: 4; y = y_hi * 4 + y_lo), z: 8, core: 2. Of those that a mesh axis runs over, the one named last changes fastest.
Arguments:
- orbitals: bfloat16 [8192, 8192], P(('row', 'col')), may hold values from -0.0625 to 0.0625
- targets: bfloat16 [8192, 1024], P(('row', 'col')), may hold values from -6 to 6
- coulomb: float32 [8192, 8192], P('row', 'col')
Outputs:
- applied: float32 [8192, 1024], P(('row', 'col'))
All inputs are finite; a program needn't handle non-finite values.
Results may differ from a plain program's by a relative error of at most 0.005.
Values may be sent and summed in bfloat16 or wider, within the bound.
A program may use at most 64 MiB of HBM per device.

v0:
```python
import jax
import jax.numpy as jnp
from jax import lax
from jax.sharding import PartitionSpec as P


def pair_tile(left, right):
    return lax.dot_general(
        left, right, (((1,), (1,)), ((), ())), preferred_element_type=jnp.float32
    )


def body(orbitals, targets, coulomb):
    col_orbs, col_targets = (
        lax.all_gather(orbitals, "row", axis=0, tiled=True),
        lax.all_gather(targets, "row", axis=0, tiled=True),
    )
    screened = (
        pair_tile(lax.all_gather(orbitals, "col", axis=0, tiled=True), col_orbs) * coulomb
    ).astype(jnp.bfloat16)
    partial_rows = jnp.dot(screened, col_targets, preferred_element_type=jnp.float32)
    return lax.psum_scatter(partial_rows, "col", scatter_dimension=0, tiled=True)


def solution(mesh):
    in_specs = (P(("row", "col"), None), P(("row", "col"), None), P("row", "col"))
    out_specs = P(("row", "col"), None)
    return jax.shard_map(body, mesh=mesh, in_specs=in_specs, out_specs=out_specs, check_vma=False)
```

profile of v0, /device:TPU:2, one launch (start us, length us, event | category | flops | bytes accessed | tf_op | source)
XLA Modules:
  0.0 445.3 jit_solution(3718126433628568119)
XLA Ops:
  6.5 0.0 all-gather.5.cloned.1.call-start
  6.5 0.7 all-gather.5.cloned.1.call-update
  7.3 0.0 all-gather.3.cloned.1.call-start
  7.3 0.7 all-gather.3.cloned.1.call-update
  8.0 0.0 reduce-scatter.2.cloned.1.call-start
  8.1 36.6 %all_gather.11 = bf16[256,1024]{1,0:T(8,128)(2,1)S(1)} all-gather(bf16[16,1024]{1,0:T(8,128)(2,1)} %param.4), channel_id=1, replica_groups=mesh['row'=16,'col'=32] {'row'}, dimensions={0}, use_global_device_ids=true | all-gather | bytes 557056 | tf_op jit(solution)/shard_map/all_gather | solution.py:16
  44.6 55.9 %all-gather.5.cloned.1.call-done = bf16[256,8192]{1,0:T(8,128)(2,1)} async-done(((bf16[16,8192]{1,0:T(8,128)(2,1)}), bf16[256,8192]{1,0:T(8,128)(2,1)}) %all-gather.5.cloned.1.call-update) | async-done | bytes 4194320 | tf_op jit(solution)/shard_map/all_gather | solution.py:15
  100.6 168.7 %all-gather.3.cloned.1.call-done = bf16[512,8192]{1,0:T(8,128)(2,1)} async-done(((bf16[16,8192]{1,0:T(8,128)(2,1)}), bf16[512,8192]{1,0:T(8,128)(2,1)}) %all-gather.3.cloned.1.call-update) | async-done | bytes 8388624 | tf_op jit(solution)/shard_map/all_gather | solution.py:19
  269.3 9.2 %fusion.1 = f32[512,1024]{1,0:T(8,128)} fusion(bf16[256,1024]{1,0:T(8,128)(2,1)S(1)} %all_gather.11, f32[512,256]{1,0:T(8,128)} %param.5, bf16[512,8192]{1,0:T(8,128)(2,1)} %all-gather.3.cloned.1.call-done, bf16[256,8192]{1,0:T(8,128)(2,1)} %all-gather.5.cloned.1.call-done), kind=kOutput, calls=%fused_computation.2 | convolution fusion | flops 2416181248 | bytes 15728640 | tf_op jit(solution)/shard_map/dot_general | solution.py:21
  278.5 0.0 reduce-scatter.2.cloned.1.call-update
  278.5 160.3 %reduce-scatter.2.cloned.1.call-done = f32[16,1024]{1,0:T(8,128)} async-done(((f32[512,1024]{1,0:T(8,128)}), f32[16,1024]{1,0:T(8,128)}) %reduce-scatter.2.cloned.1.call-update) | async-done | bytes 65552 | tf_op jit(solution)/shard_map/reduce_scatter | solution.py:22
Async XLA Ops:
  6.5 94.0 %all-gather.5.cloned.1.call-start = ((), (), s32[]{:S(2)}) async-start(), calls=%async_computation.2 | async-start | bytes 4456448 | tf_op jit(solution)/shard_map/all_gather | solution.py:15
  7.3 262.0 %all-gather.3.cloned.1.call-start = ((), (), s32[]{:S(2)}) async-start(), calls=%async_computation.1 | async-start | bytes 8650752 | tf_op jit(solution)/shard_map/all_gather | solution.py:19
  8.0 430.8 %reduce-scatter.2.cloned.1.call-start = ((), (), s32[]{:S(2)}) async-start(), calls=%async_computation.3 | async-start | bytes 2162688 | tf_op jit(solution)/shard_map/reduce_scatter | solution.py:22
Sparse Core Ops, SparseCore 0:
  10.6 89.8 all-gather.4
  102.6 166.6 all-gather.2
  278.6 160.1 reduce-scatter.1
where the time goes:
time: 445 us
  waiting for transfers between devices  386 us (87%)
  blocking collectives  36.6 us (8%)
  between operations  13.1 us (3%)
  matrix products  9.19 us (2%)
    all_gather x1, waiting for transfers between devices, body(): lax.all_gather(orbitals, 'col', axis=0, tiled=True)  169 us
    reduce_scatter x1, waiting for transfers between devices, body(): lax.psum_scatter(partial_rows, 'col', scatter_dimension=0, tiled=True)  160 us
    all_gather x1, waiting for transfers between devices, body(): lax.all_gather(orbitals, 'row', axis=0, tiled=True)  55.9 us
    all_gather x1, blocking collectives, body(): lax.all_gather(targets, 'row', axis=0, tiled=True)  36.6 us
    dot_general x1, matrix products, body(): jnp.dot(screened, col_targets, preferred_element_type=jnp.float32)  9.19 us
  transfers between devices with their start and end apart: 3, of which 3 were waited for; matrix products, arithmetic and copies ran while one was open for 0% of the time, Pallas kernels for 0%

commit v1 on v0

v1 whole, which is shorter than its diff:
```python
import functools

import jax
import jax.numpy as jnp
from jax import lax
from jax.experimental import pallas as pl
from jax.experimental.pallas import tpu as pltpu
from jax.sharding import PartitionSpec as P

MESH = pl.DeviceIdType.MESH
F32 = jnp.float32
BF16 = jnp.bfloat16
KS = 1024
NB = 1024

SLOT = {4: 0, 0: 1, 1: 2, -1: 3, 2: 4, -2: 5, 3: 6, -3: 7, -4: 0}
OFFSET = (4, 0, 1, -1, 2, -2, 3, -3)
RECTS = ((1, 6, 1, 6), (6, 8, 1, 8), (1, 6, 6, 8), (0, 1, 0, 8), (1, 8, 0, 1))
DX = (0, 1, 3, 2)


def kernel(
    orb, tgt, cou, out,
    A, B, T, SB, RB, OWN, XS, XR, VF, VB, VR, S, OB, OR, OO,
    loc, a_s, a_r, g_s, g_r, t_s, t_r, v_s, v_r, d_s, d_r, x_s, x_r, o_s, o_r,
):
    row, col = lax.axis_index("row"), lax.axis_index("col")
    x, yh, c = lax.div(row, 4), lax.rem(lax.div(row, 2), 2), lax.rem(row, 2)
    yl, z = lax.div(col, 8), lax.rem(col, 8)
    y = yh * 4 + yl
    sib = 1 - c

    def dev(x_, y_, z_, c_):
        return ((x_ * 2 + lax.div(y_, 4)) * 2 + c_, lax.rem(y_, 4) * 8 + z_)

    def at(dx=0, dy=0, dz=0, dc=0):
        return dev(
            lax.rem(x + dx + 4, 4), lax.rem(y + dy + 8, 8), lax.rem(z + dz + 8, 8), sib if dc else c
        )

    def yl_peer(d):
        return (row, lax.rem(yl + d, 4) * 8 + z)

    started = []

    def remote(src, dst, ss, rs, to):
        return pltpu.make_async_remote_copy(
            src_ref=src, dst_ref=dst, send_sem=ss, recv_sem=rs, device_id=to, device_id_type=MESH
        )

    def go(cp):
        cp.start()
        started.append(cp)
        return cp

    own_slice = lambda g: orb.at[:, pl.ds(pl.multiple_of(g * KS, KS), KS)]

    v_in = pltpu.make_async_copy(cou, VF, loc.at[0])
    v_in.start()
    t_in = pltpu.make_async_copy(tgt, T.at[1, x, c], loc.at[1])
    t_in.start()
    a_in = pltpu.make_async_copy(own_slice(x * 2 + c), A.at[1, x, c], loc.at[2])
    a_in.start()

    barrier = pltpu.get_barrier_semaphore()
    partners = [at(dx=dx, dc=dc) for dx in range(4) for dc in range(2) if dx or dc]
    partners += [at(dy=1), at(dy=-1)] + [at(dz=d) for d in range(1, 8)] + [yl_peer(d) for d in (1, 2, 3)]
    for p in partners:
        pl.semaphore_signal(barrier, inc=1, device_id=p, device_id_type=MESH)
    pl.semaphore_wait(barrier, len(partners))

    swaps = {}
    for i, dx in enumerate(DX):
        for dc in (1, 0):
            if dx or dc:
                n = dx * 2 + dc - 1
                xp = lax.rem(x + dx, 4)
                cp_ = sib if dc else c
                swaps[dx, dc] = go(
                    remote(own_slice(xp * 2 + cp_), A.at[1, x, c], a_s.at[n], a_r.at[n], at(dx=dx, dc=dc))
                )

    def t_ring(d, s):
        sg = -1 if d == 0 else 1
        src = tgt if s == 1 else T.at[SLOT[sg * (s - 1)], x, c]
        n = d * 4 + s - 1
        return remote(src, T.at[SLOT[sg * s], x, c], t_s.at[n], t_r.at[n], at(dy=-sg))

    tr = {(d, 1): go(t_ring(d, 1)) for d in (0, 1)}

    chunk = [lax.rem(x - dx + 4, 4) for dx in DX]

    def ring(kind, d, s, i):
        sg = -1 if d == 0 else 1
        buf = B if kind else A
        src = A if s == 1 else buf
        n = ((kind * 2 + d) * 4 + s - 1) * 4 + i
        to = at(dy=-sg) if kind else at(dz=-sg)
        return remote(
            src.at[SLOT[sg * (s - 1)], chunk[i]], buf.at[SLOT[sg * s], chunk[i]], g_s.at[n], g_r.at[n], to
        )

    rg = {}

    def forward(s, i):
        for kind in (1, 0):
            for d in (0, 1):
                if s > 1:
                    rg[kind, d, s - 1, i].wait_recv()
                if s < 4 or (d == 0) == (i < 2):
                    rg[kind, d, s, i] = go(ring(kind, d, s, i))

    b_own = []
    for i, dx in enumerate(DX):
        if dx == 0:
            a_in.wait()
            swaps[0, 1].wait_recv()
        else:
            swaps[dx, 0].wait_recv()
            swaps[dx, 1].wait_recv()
        forward(1, i)
        cp = pltpu.make_async_copy(A.at[1, chunk[i]], B.at[1, chunk[i]], loc.at[3 + i])
        cp.start()
        b_own.append(cp)

    def t_forward(s):
        for d in (0, 1):
            if (d, s - 1) in tr:
                tr[d, s - 1].wait_recv()
            if s < 4 or d == 0:
                if s < 5:
                    tr[d, s] = go(t_ring(d, s))

    t_forward(2)

    v_in.wait()
    dst = lax.broadcasted_iota(jnp.int32, (256, 256), 1)
    src = lax.broadcasted_iota(jnp.int32, (256, 256), 0)
    want = ((dst & 127) >> 5) * 64 + (dst >> 7) * 32 + (dst & 31)
    perm = jnp.where(src == want, 1.0, 0.0).astype(BF16)
    for q in range(4):
        moved = jnp.dot(VF[q * 128:(q + 1) * 128, :].astype(BF16), perm, preferred_element_type=F32).astype(BF16)
        VB[q, 0] = moved[:, :128].reshape(8, 16, 128)
        VB[q, 1] = moved[:, 128:].reshape(8, 16, 128)
    v_own = pltpu.make_async_copy(VB.at[yl], VR.at[yl], loc.at[7])
    v_own.start()

    dd, xx = {}, {}

    def compute(n):
        r0, r1, c0, c1 = RECTS[n]
        rows = (r1 - r0) * 64
        for half in (0, 1):
            left = A[r0:r1, :, c if half else sib].reshape(rows, KS)
            q = c0
            while q < c1:
                w = min(2 - (q & 1), c1 - q)
                right = B[q:q + w].reshape(w * 128, KS)
                tile = lax.dot_general(left, right, (((1,), (1,)), ((), ())), preferred_element_type=F32)
                tile = tile.reshape(r1 - r0, 4, 16, w * 128)
                if half:
                    OWN[r0:r1, :, :, q * 128:(q + w) * 128] = tile
                else:
                    SB[r0:r1, :, :, q * 128:(q + w) * 128] = tile.astype(BF16)
                q += w
            if not half:
                where = (slice(r0, r1), slice(None), slice(None), slice(c0 * 128, c1 * 128))
                dd[n] = go(remote(SB.at[where], RB.at[where], d_s.at[n], d_r.at[n], at(dc=1)))

    def combine(n):
        r0, r1, c0, c1 = RECTS[n]
        cols = slice(c0 * 128, c1 * 128)
        dd[n].wait_recv()
        for dx in (2, 1, 3):
            xp = lax.rem(x + dx, 4)
            for r in range(r0, r1):
                XS[dx - 1, r, :, cols] = (OWN[r, xp, :, cols] + RB[r, xp, :, cols].astype(F32)).astype(BF16)
            k = n * 3 + dx - 1
            where = (dx - 1, slice(r0, r1), slice(None), cols)
            xx[n, dx] = go(remote(XS.at[where], XR.at[where], x_s.at[k], x_r.at[k], at(dx=dx)))

    def finish(n):
        r0, r1, c0, c1 = RECTS[n]
        for dx in (1, 2, 3):
            xx[n, dx].wait_recv()
        for q in range(c0, c1):
            yq = lax.rem(y + OFFSET[q] + 8, 8)
            cols = slice(q * 128, (q + 1) * 128)
            for r in range(r0, r1):
                zr = lax.rem(z + OFFSET[r] + 8, 8)
                pairs = OWN[r, x, :, cols] + RB[r, x, :, cols].astype(F32)
                for k in range(3):
                    pairs = pairs + XR[k, r, :, cols].astype(F32)
                v = VR[lax.rem(yq, 4), lax.div(yq, 4), zr].astype(F32)
                S[r, :, cols] = (pairs * v).astype(BF16)

    xm, xp1, xf = lax.rem(x + 3, 4), lax.rem(x + 1, 4), lax.rem(x + 2, 4)
    tx, td = {}, {}

    def t_sib(k, xv):
        td[k] = go(remote(T.at[:, xv, c], T.at[:, xv, c], t_s.at[12 + k], t_r.at[12 + k], at(dc=1)))

    def t_first():
        tx[0] = go(remote(T.at[:, x, c], T.at[:, x, c], t_s.at[8], t_r.at[8], at(dx=1)))
        tx[1] = go(remote(T.at[:, x, c], T.at[:, x, c], t_s.at[9], t_r.at[9], at(dx=-1)))
        t_sib(0, x)

    def t_second():
        tx[0].wait_recv()
        tx[2] = go(remote(T.at[0:4, xm, c], T.at[0:4, xm, c], t_s.at[10], t_r.at[10], at(dx=1)))
        tx[1].wait_recv()
        tx[3] = go(remote(T.at[4:8, xp1, c], T.at[4:8, xp1, c], t_s.at[11], t_r.at[11], at(dx=-1)))
        t_sib(1, xm)
        t_sib(2, xp1)

    def t_third():
        tx[2].wait_recv()
        tx[3].wait_recv()
        t_sib(3, xf)

    for i in range(4):
        forward(2, i)
        if i == 0:
            t_forward(3)
        if i == 2:
            t_forward(4)
    t_forward(5)
    t_in.wait()
    t_first()
    for i in range(4):
        forward(3, i)
    for cp in b_own:
        cp.wait()
    compute(0)
    for i in range(4):
        forward(4, i)
        if i == 1:
            combine(0)
    t_second()
    v_out = []
    for d in (1, 2, 3):
        v_out.append(
            go(remote(VB.at[lax.rem(yl + d, 4)], VR.at[yl], v_s.at[d - 1], v_r.at[d - 1], yl_peer(d)))
        )
    compute(1)
    compute(2)
    combine(1)
    combine(2)
    t_third()
    for i in range(4):
        for kind in (1, 0):
            rg[kind, 0 if i < 2 else 1, 4, i].wait_recv()
    compute(3)
    compute(4)
    combine(3)
    combine(4)
    v_own.wait()
    for cp in v_out:
        cp.wait_recv()
    for n in range(5):
        finish(n)
    for k in range(4):
        td[k].wait_recv()

    left = S[...].reshape(128, 1024)
    for q in range(4):
        cols = slice(q * 256, (q + 1) * 256)
        part = jnp.dot(left, T[:, :, :, :, cols].reshape(1024, 256), preferred_element_type=F32)
        part = part.reshape(8, 16, 256)
        OO[:, cols] = part[1]
        OB[:, :, cols] = part.astype(BF16)
    oo = []
    for o in (4, 3, -3, 2, -2, 1, -1):
        s = SLOT[o]
        n = s if s == 0 else s - 1
        oo.append(go(remote(OB.at[s], OR.at[n], o_s.at[n], o_r.at[n], at(dz=o))))
    for cp in oo:
        cp.wait_recv()
    total = OO[...]
    for n in range(7):
        total = total + OR[n].astype(F32)
    out[...] = total
    for cp in started:
        cp.wait_send()


def body(orbitals, targets, coulomb):
    any_, dma = pl.BlockSpec(memory_space=pl.ANY), pltpu.SemaphoreType.DMA
    return pl.pallas_call(
        kernel,
        out_shape=jax.ShapeDtypeStruct((16, NB), F32),
        in_specs=[any_] * 3,
        out_specs=pl.BlockSpec(memory_space=pltpu.VMEM),
        scratch_shapes=[
            pltpu.VMEM((8, 4, 2, 16, KS), BF16),
            pltpu.VMEM((8, 4, 2, 16, KS), BF16),
            pltpu.VMEM((8, 4, 2, 16, NB), BF16),
            pltpu.VMEM((8, 4, 16, 1024), BF16),
            pltpu.VMEM((8, 4, 16, 1024), BF16),
            pltpu.VMEM((8, 4, 16, 1024), F32),
            pltpu.VMEM((3, 8, 16, 1024), BF16),
            pltpu.VMEM((3, 8, 16, 1024), BF16),
            pltpu.VMEM((512, 256), F32),
            pltpu.VMEM((4, 2, 8, 16, 128), BF16),
            pltpu.VMEM((4, 2, 8, 16, 128), BF16),
            pltpu.VMEM((8, 16, 1024), BF16),
            pltpu.VMEM((8, 16, NB), BF16),
            pltpu.VMEM((7, 16, NB), BF16),
            pltpu.VMEM((16, NB), F32),
            dma((8,)),
            dma((7,)), dma((7,)),
            dma((64,)), dma((64,)),
            dma((16,)), dma((16,)),
            dma((3,)), dma((3,)),
            dma((5,)), dma((5,)),
            dma((15,)), dma((15,)),
            dma((7,)), dma((7,)),
        ],
        compiler_params=pltpu.CompilerParams(
            collective_id=0, has_side_effects=True, vmem_limit_bytes=40 * 1024 * 1024
        ),
        cost_estimate=pl.CostEstimate(flops=2_500_000_000, bytes_accessed=4_000_000, transcendentals=0),
    )(orbitals, targets, coulomb)


def solution(mesh):
    in_specs = (P(("row", "col"), None), P(("row", "col"), None), P("row", "col"))
    return jax.shard_map(
        body, mesh=mesh, in_specs=in_specs, out_specs=P(("row", "col"), None), check_vma=False
    )
```

time: 445 us -> 70.4 us (0.16)
  the two profiles are of different devices: /device:TPU:2 before, /device:TPU:1 now
where the time goes in v1:
time: 70.4 us; the launch traced here: 70.1 us
  Pallas kernels  66.7 us (95%)
  local copies, waits for them, and re-layouts  3.38 us (5%)
    pallas_call x1, Pallas kernels, body(): pl.pallas_call(kernel, out_shape=jax.ShapeDtypeStruct((16, NB), F32), in_...  66.7 us
    unnamed x7, local copies, waits for them, and re-layouts  3.38 us

profile of v1, /device:TPU:1, one launch (start us, length us, event | category | flops | bytes accessed | tf_op | source)
XLA Modules:
  0.0 70.1 jit_solution(233354475476062230)
XLA Ops:
  0.0 0.0 copy-start
  0.0 1.0 %copy-done = f32[512,256]{1,0:T(8,128)S(1)} copy-done((f32[512,256]{1,0:T(8,128)S(1)}, f32[512,256]{1,0:T(8,128)}, u32[]{:S(2)}) %copy-start) | copy-done | bytes 524312
  1.0 0.0 copy-start.1
  1.0 0.9 %copy-done.1 = bf16[16,8192]{1,0:T(8,128)(2,1)S(1)} copy-done((bf16[16,8192]{1,0:T(8,128)(2,1)S(1)}, bf16[16,8192]{1,0:T(8,128)(2,1)}, u32[]{:S(2)}) %copy-start.1) | copy-done | bytes 262168
  2.0 0.0 copy-start.2
  2.0 0.8 %copy-done.2 = bf16[16,1024]{1,0:T(8,128)(2,1)S(1)} copy-done((bf16[16,1024]{1,0:T(8,128)(2,1)S(1)}, bf16[16,1024]{1,0:T(8,128)(2,1)}, u32[]{:S(2)}) %copy-start.2) | copy-done | bytes 32792
  2.8 66.7 %shard_map.37 = f32[16,1024]{1,0:T(8,128)S(1)} custom-call(bf16[16,8192]{1,0:T(8,128)(2,1)S(1)} %copy-done.1, bf16[16,1024]{1,0:T(8,128)(2,1)S(1)} %copy-done.2, f32[512,256]{1,0:T(8,128)S(1)} %copy-done), custom_call_target="tpu_custom_call" | custom-call | flops 2500000000 | bytes 4000000 | tf_op jit(solution)/shard_map/pallas_call | solution.py:289
  69.5 0.6 copy.5
Async XLA Ops:
  0.0 1.0 %copy-start = (f32[512,256]{1,0:T(8,128)S(1)}, f32[512,256]{1,0:T(8,128)}, u32[]{:S(2)}) copy-start(f32[512,256]{1,0:T(8,128)} %cou.1) | copy-start | bytes 1572868
  1.0 0.9 %copy-start.1 = (bf16[16,8192]{1,0:T(8,128)(2,1)S(1)}, bf16[16,8192]{1,0:T(8,128)(2,1)}, u32[]{:S(2)}) copy-start(bf16[16,8192]{1,0:T(8,128)(2,1)} %orb.1) | copy-start | bytes 786436
  2.0 0.8 %copy-start.2 = (bf16[16,1024]{1,0:T(8,128)(2,1)S(1)}, bf16[16,1024]{1,0:T(8,128)(2,1)}, u32[]{:S(2)}) copy-start(bf16[16,1024]{1,0:T(8,128)(2,1)} %tgt.1) | copy-start | bytes 98308

commit v2 on v1

v2 whole, which is shorter than its diff:
```python
import functools

import jax
import jax.numpy as jnp
from jax import lax
from jax.experimental import pallas as pl
from jax.experimental.pallas import tpu as pltpu
from jax.sharding import PartitionSpec as P

MESH = pl.DeviceIdType.MESH
F32 = jnp.float32
BF16 = jnp.bfloat16
KS = 1024
NB = 1024

SLOT = {4: 0, 0: 1, 1: 2, -1: 3, 2: 4, -2: 5, 3: 6, -3: 7, -4: 0}
OFFSET = (4, 0, 1, -1, 2, -2, 3, -3)
RECTS = ((1, 6, 1, 6), (6, 8, 1, 8), (1, 6, 6, 8), (0, 1, 1, 8), (0, 8, 0, 1))
HALVES = (
    ((slice(1, 4), slice(128, 768)), (slice(4, 6), slice(128, 768))),
    ((slice(6, 7), slice(128, 1024)), (slice(7, 8), slice(128, 1024))),
    ((slice(1, 6), slice(768, 896)), (slice(1, 6), slice(896, 1024))),
)
DX = (0, 1, 3, 2)


def kernel(
    orb, tgt, cou, out,
    W, A, B, T, SB, RB, OWN, XS, XR, YS, YR, VF, VB, VR, S, OB, OA, OH, OC, OR, OO,
    loc, a_s, a_r, g_s, g_r, t_s, t_r, v_s, v_r, d_s, d_r, x_s, x_r, o_s, o_r,
):
    row, col = lax.axis_index("row"), lax.axis_index("col")
    x, yh, c = lax.div(row, 4), lax.rem(lax.div(row, 2), 2), lax.rem(row, 2)
    yl, z = lax.div(col, 8), lax.rem(col, 8)
    y = yh * 4 + yl
    sib = 1 - c

    def dev(x_, y_, z_, c_):
        return ((x_ * 2 + lax.div(y_, 4)) * 2 + c_, lax.rem(y_, 4) * 8 + z_)

    def at(dx=0, dy=0, dz=0, dc=0):
        return dev(
            lax.rem(x + dx + 4, 4), lax.rem(y + dy + 8, 8), lax.rem(z + dz + 8, 8), sib if dc else c
        )

    def yl_peer(d):
        return (row, lax.rem(yl + d, 4) * 8 + z)

    started = []
    tr = {}

    def remote(src, dst, ss, rs, to):
        return pltpu.make_async_remote_copy(
            src_ref=src, dst_ref=dst, send_sem=ss, recv_sem=rs, device_id=to, device_id_type=MESH
        )

    def go(cp):
        cp.start()
        started.append(cp)
        return cp

    def own_slice(ref, g):
        return ref.at[:, pl.ds(pl.multiple_of(g * KS, KS), KS)]

    w_in = pltpu.make_async_copy(orb, W, loc.at[8])
    w_in.start()
    v_in = pltpu.make_async_copy(cou, VF, loc.at[0])
    v_in.start()
    t_in = pltpu.make_async_copy(tgt, T.at[1, x, c], loc.at[1])
    t_in.start()
    a_in = pltpu.make_async_copy(own_slice(orb, x * 2 + c), A.at[1, x, c], loc.at[2])
    a_in.start()

    barrier = pltpu.get_barrier_semaphore()
    partners = [at(dx=dx, dc=dc) for dx in range(4) for dc in range(2) if dx or dc]
    partners += [at(dy=d) for d in (1, -1, 2, -2)] + [at(dz=d) for d in (1, -1, 2, -2)] + [yl_peer(d) for d in (1, 2, 3)]
    for p in partners:
        pl.semaphore_signal(barrier, inc=1, device_id=p, device_id_type=MESH)
    pl.semaphore_wait(barrier, len(partners))

    def t_send(n, d, src, dst, cols, far):
        cp = remote(
            T.at[SLOT[src], x, c, :, cols], T.at[SLOT[dst], x, c, :, cols], t_s.at[n], t_r.at[n],
            at(dy=far * (1 - 2 * d)),
        )
        tr[n] = go(cp)

    whole, half = slice(0, NB), (slice(0, NB // 2), slice(NB // 2, NB))

    def t_start():
        for d in (0, 1):
            sg = 2 * d - 1
            t_send(d, d, 0, 2 * sg, whole, 2)
            t_send(2 + d, d, 0, sg, whole, 1)

    def t_on():
        for d in (0, 1):
            sg = 2 * d - 1
            tr[d].wait_recv()
            t_send(4 + d, d, 2 * sg, 3 * sg, whole, 1)
            t_send(6 + d, d, 2 * sg, 4 * sg, half[d], 2)

    swaps = {}
    w_in.wait()
    t_in.wait()
    for i, dx in enumerate(DX):
        for dc in (1, 0):
            if dx or dc:
                n = dx * 2 + dc - 1
                xp = lax.rem(x + dx, 4)
                cp_ = sib if dc else c
                swaps[dx, dc] = go(
                    remote(own_slice(W, xp * 2 + cp_), A.at[1, x, c], a_s.at[n], a_r.at[n], at(dx=dx, dc=dc))
                )

    t_start()

    chunk = [lax.rem(x - dx + 4, 4) for dx in DX]

    def ring(kind, d, s, i):
        sg = -1 if d == 0 else 1
        buf = B if kind else A
        src = A if s == 1 else buf
        n = ((kind * 2 + d) * 4 + s - 1) * 4 + i
        to = at(dy=-sg) if kind else at(dz=-sg)
        return remote(
            src.at[SLOT[sg * (s - 1)], chunk[i]], buf.at[SLOT[sg * s], chunk[i]], g_s.at[n], g_r.at[n], to
        )

    rg = {}

    def forward(s, i):
        for kind in (1, 0):
            for d in (0, 1):
                if s > 1:
                    rg[kind, d, s - 1, i].wait_recv()
                if s < 4 or (d == 0) == (i < 2):
                    rg[kind, d, s, i] = go(ring(kind, d, s, i))

    b_own = []
    for i, dx in enumerate(DX):
        if dx == 0:
            a_in.wait()
            swaps[0, 1].wait_recv()
        else:
            swaps[dx, 0].wait_recv()
            swaps[dx, 1].wait_recv()
        forward(1, i)
        cp = pltpu.make_async_copy(A.at[1, chunk[i]], B.at[1, chunk[i]], loc.at[3 + i])
        cp.start()
        b_own.append(cp)
    t_on()

    v_in.wait()
    dst = lax.broadcasted_iota(jnp.int32, (256, 256), 1)
    src = lax.broadcasted_iota(jnp.int32, (256, 256), 0)
    want = ((dst & 127) >> 5) * 64 + (dst >> 7) * 32 + (dst & 31)
    perm = jnp.where(src == want, 1.0, 0.0).astype(BF16)
    for q in range(4):
        moved = jnp.dot(VF[q * 128:(q + 1) * 128, :].astype(BF16), perm, preferred_element_type=F32).astype(BF16)
        VB[q, 0] = moved[:, :128].reshape(8, 16, 128)
        VB[q, 1] = moved[:, 128:].reshape(8, 16, 128)
    v_own = pltpu.make_async_copy(VB.at[yl], VR.at[yl], loc.at[7])
    v_own.start()

    dd, xx = {}, {}

    def compute(n):
        r0, r1, c0, c1 = RECTS[n]
        rows = (r1 - r0) * 64
        left = jnp.concatenate(
            [A[r0:r1, :, sib].reshape(rows, KS), A[r0:r1, :, c].reshape(rows, KS)], axis=0
        )
        q = c0
        while q < c1:
            w = min(2 - (q & 1), c1 - q)
            right = B[q:q + w].reshape(w * 128, KS)
            tile = lax.dot_general(left, right, (((1,), (1,)), ((), ())), preferred_element_type=F32)
            tile = tile.reshape(2, r1 - r0, 4, 16, w * 128)
            cols = slice(q * 128, (q + w) * 128)
            SB[r0:r1, :, :, cols] = tile[0].astype(BF16)
            OWN[r0:r1, :, :, cols] = tile[1]
            q += w
        where = (slice(r0, r1), slice(None), slice(None), slice(c0 * 128, c1 * 128))
        dd[n] = go(remote(SB.at[where], RB.at[where], d_s.at[n], d_r.at[n], at(dc=1)))

    xm, xp1, xf = lax.rem(x + 3, 4), lax.rem(x + 1, 4), lax.rem(x + 2, 4)

    def x_send(n, k, src, dst, d, rows, cols):
        where = (d, rows, slice(None), cols)
        xx[n, k, d] = go(
            remote(src.at[where], dst.at[where], x_s.at[n * 4 + k * 2 + d], x_r.at[n * 4 + k * 2 + d], at(dx=1 - 2 * d))
        )

    def spread(n):
        dd[n].wait_recv()
        for d in (0, 1):
            rows, cols = HALVES[n][d]
            for r in range(rows.start, rows.stop):
                XS[d, r, :, cols] = (OWN[r, xf, :, cols] + RB[r, xf, :, cols].astype(F32)).astype(BF16)
            x_send(n, 0, XS, XR, d, rows, cols)

    def combine(n):
        r0, r1, c0, c1 = RECTS[n]
        for d in (0, 1):
            xx[n, 0, d].wait_recv()
            to = xm if d else xp1
            for h in (0, 1):
                rows, cols = HALVES[n][h]
                for r in range(rows.start, rows.stop):
                    part = OWN[r, to, :, cols] + RB[r, to, :, cols].astype(F32)
                    if h == d:
                        part = part + XR[d, r, :, cols].astype(F32)
                    YS[d, r, :, cols] = part.astype(BF16)
            x_send(n, 1, YS, YR, d, slice(r0, r1), slice(c0 * 128, c1 * 128))

    def direct(n):
        r0, r1, c0, c1 = RECTS[n]
        rows, cols = slice(r0, r1), slice(c0 * 128, c1 * 128)
        dd[n].wait_recv()
        for k, buf, land, to, dx in ((2, XS, XR, xf, 2), (0, YS, YR, xp1, 1), (1, YS, YR, xm, -1)):
            j = k % 2
            for r in range(r0, r1):
                buf[j, r, :, cols] = (OWN[r, to, :, cols] + RB[r, to, :, cols].astype(F32)).astype(BF16)
            where = (j, rows, slice(None), cols)
            m = n * 4 + k
            xx[n, 1, k] = go(remote(buf.at[where], land.at[where], x_s.at[m], x_r.at[m], at(dx=dx)))

    def finish(n):
        r0, r1, c0, c1 = RECTS[n]
        for d in (0, 1, 2):
            if (n, 1, d) in xx:
                xx[n, 1, d].wait_recv()
        for q in range(c0, c1):
            yq = lax.rem(y + OFFSET[q] + 8, 8)
            cols = slice(q * 128, (q + 1) * 128)
            for r in range(r0, r1):
                zr = lax.rem(z + OFFSET[r] + 8, 8)
                pairs = OWN[r, x, :, cols] + RB[r, x, :, cols].astype(F32)
                for d in (0, 1):
                    pairs = pairs + YR[d, r, :, cols].astype(F32)
                if n > 2:
                    pairs = pairs + XR[0, r, :, cols].astype(F32)
                v = VR[lax.rem(yq, 4), lax.div(yq, 4), zr].astype(F32)
                S[r, :, cols] = (pairs * v).astype(BF16)

    tx, td = {}, {}

    def t_sib(k, xv):
        td[k] = go(remote(T.at[:, xv, c], T.at[:, xv, c], t_s.at[12 + k], t_r.at[12 + k], at(dc=1)))

    def t_first():
        for n in range(2, 8):
            tr[n].wait_recv()
        tx[0] = go(remote(T.at[:, x, c], T.at[:, x, c], t_s.at[8], t_r.at[8], at(dx=1)))
        tx[1] = go(remote(T.at[:, x, c], T.at[:, x, c], t_s.at[9], t_r.at[9], at(dx=-1)))
        t_sib(0, x)

    def t_second():
        tx[0].wait_recv()
        tx[2] = go(remote(T.at[0:4, xm, c], T.at[0:4, xm, c], t_s.at[10], t_r.at[10], at(dx=1)))
        tx[1].wait_recv()
        tx[3] = go(remote(T.at[4:8, xp1, c], T.at[4:8, xp1, c], t_s.at[11], t_r.at[11], at(dx=-1)))
        t_sib(1, xm)
        t_sib(2, xp1)

    def t_third():
        tx[2].wait_recv()
        tx[3].wait_recv()
        t_sib(3, xf)

    for i in range(4):
        forward(2, i)
    t_first()
    for i in range(4):
        forward(3, i)
    for cp in b_own:
        cp.wait()
    compute(0)
    for i in range(4):
        forward(4, i)
        if i == 0:
            spread(0)
            t_second()
    compute(1)
    compute(2)
    combine(0)
    spread(1)
    spread(2)
    for i in range(4):
        rg[0, i // 2, 4, i].wait_recv()
    compute(3)
    for i in range(4):
        rg[1, i // 2, 4, i].wait_recv()
    v_out = []
    for d in (1, 2, 3):
        v_out.append(
            go(remote(VB.at[lax.rem(yl + d, 4)], VR.at[yl], v_s.at[d - 1], v_r.at[d - 1], yl_peer(d)))
        )
    compute(4)
    direct(3)
    direct(4)
    combine(1)
    combine(2)
    t_third()
    v_own.wait()
    for cp in v_out:
        cp.wait_recv()
    for n in range(5):
        finish(n)
    for k in range(4):
        td[k].wait_recv()

    left = S[...].reshape(128, 1024)
    for q in range(4):
        cols = slice(q * 256, (q + 1) * 256)
        part = jnp.dot(left, T[:, :, :, :, cols].reshape(1024, 256), preferred_element_type=F32)
        part = part.reshape(8, 16, 256)
        for k in range(3):
            OO[k, :, cols] = part[SLOT[(0, 2, -2)[k]]]
        OB[:, :, cols] = part.astype(BF16)

    def o_send(n, src, dst, dz):
        return go(remote(src, dst, o_s.at[n], o_r.at[n], at(dz=dz)))

    far = [o_send(d, OB.at[0, :, half[d]], OH.at[d], 2 - 4 * d) for d in (0, 1)]
    far += [o_send(2 + d, OB.at[SLOT[3 - 6 * d]], OA.at[d], 1 - 2 * d) for d in (0, 1)]
    near = [o_send(4 + d, OB.at[SLOT[1 - 2 * d]], OR.at[d], 1 - 2 * d) for d in (0, 1)]
    for d in (0, 1):
        far[d].wait_recv()
        far[2 + d].wait_recv()
        for h in (0, 1):
            joined = OO[1 + d, :, half[h]] + OA[d, :, half[h]].astype(F32)
            if h == d:
                joined = joined + OH[d].astype(F32)
            OC[d, :, half[h]] = joined.astype(BF16)
        near.append(o_send(6 + d, OC.at[d], OR.at[2 + d], 2 - 4 * d))
    total = OO[0]
    for n in range(4):
        near[n].wait_recv()
        total = total + OR[n].astype(F32)
    out[...] = total
    for cp in started:
        cp.wait_send()


def body(orbitals, targets, coulomb):
    any_, dma = pl.BlockSpec(memory_space=pl.ANY), pltpu.SemaphoreType.DMA
    return pl.pallas_call(
        kernel,
        out_shape=jax.ShapeDtypeStruct((16, NB), F32),
        in_specs=[any_] * 3,
        out_specs=pl.BlockSpec(memory_space=pltpu.VMEM),
        scratch_shapes=[
            pltpu.VMEM((16, 8 * KS), BF16),
            pltpu.VMEM((8, 4, 2, 16, KS), BF16),
            pltpu.VMEM((8, 4, 2, 16, KS), BF16),
            pltpu.VMEM((8, 4, 2, 16, NB), BF16),
            pltpu.VMEM((8, 4, 16, 1024), BF16),
            pltpu.VMEM((8, 4, 16, 1024), BF16),
            pltpu.VMEM((8, 4, 16, 1024), F32),
            pltpu.VMEM((2, 8, 16, 1024), BF16),
            pltpu.VMEM((2, 8, 16, 1024), BF16),
            pltpu.VMEM((2, 8, 16, 1024), BF16),
            pltpu.VMEM((2, 8, 16, 1024), BF16),
            pltpu.VMEM((512, 256), F32),
            pltpu.VMEM((4, 2, 8, 16, 128), BF16),
            pltpu.VMEM((4, 2, 8, 16, 128), BF16),
            pltpu.VMEM((8, 16, 1024), BF16),
            pltpu.VMEM((8, 16, NB), BF16),
            pltpu.VMEM((2, 16, NB), BF16),
            pltpu.VMEM((2, 16, NB // 2), BF16),
            pltpu.VMEM((2, 16, NB), BF16),
            pltpu.VMEM((4, 16, NB), BF16),
            pltpu.VMEM((3, 16, NB), F32),
            dma((9,)),
            dma((7,)), dma((7,)),
            dma((64,)), dma((64,)),
            dma((16,)), dma((16,)),
            dma((3,)), dma((3,)),
            dma((5,)), dma((5,)),
            dma((20,)), dma((20,)),
            dma((8,)), dma((8,)),
        ],
        compiler_params=pltpu.CompilerParams(
            collective_id=0, has_side_effects=True, vmem_limit_bytes=60 * 1024 * 1024
        ),
        cost_estimate=pl.CostEstimate(flops=2_500_000_000, bytes_accessed=4_000_000, transcendentals=0),
    )(orbitals, targets, coulomb)


def solution(mesh):
    in_specs = (P(("row", "col"), None), P(("row", "col"), None), P("row", "col"))
    return jax.shard_map(
        body, mesh=mesh, in_specs=in_specs, out_specs=P(("row", "col"), None), check_vma=False
    )
```

time: 70.4 us -> 62.5 us (0.89)
  Pallas kernels: 66.7 us -> 60.5 us
  local copies, waits for them, and re-layouts: 3.38 us -> 1.47 us
    pallas_call x1, Pallas kernels: 66.7 us -> 60.5 us  [body(): pl.pallas_call(kernel, out_shape=jax.ShapeDtypeStruct((16, NB), F32), in_...]
    unnamed x7 -> x1, local copies, waits for them, and re-layouts: 3.38 us -> 1.47 us
where the time goes in v2:
time: 62.5 us; the launch traced here: 62 us
  Pallas kernels  60.5 us (97%)
  local copies, waits for them, and re-layouts  1.47 us (2%)
    pallas_call x1, Pallas kernels, body(): pl.pallas_call(kernel, out_shape=jax.ShapeDtypeStruct((16, NB), F32), in_...  60.5 us
    unnamed x1, local copies, waits for them, and re-layouts  1.47 us

profile of v2, /device:TPU:1, one launch (start us, length us, event | category | flops | bytes accessed | tf_op | source)
XLA Modules:
  0.0 62.0 jit_solution(3173185668008447679)
XLA Ops:
  0.0 60.5 %shard_map.37 = f32[16,1024]{1,0:T(8,128)} custom-call(bf16[16,8192]{1,0:T(8,128)(2,1)} %orb.1, bf16[16,1024]{1,0:T(8,128)(2,1)} %tgt.1, f32[512,256]{1,0:T(8,128)} %cou.1), custom_call_target="tpu_custom_call" | custom-call | flops 2500000000 | bytes 4000000 | tf_op jit(solution)/shard_map/pallas_call | solution.py:349
  60.5 1.5 %copy.5 = f32[16,1024]{1,0:T(8,128)} copy(f32[16,1024]{1,0:T(8,128)} %shard_map.37) | data formatting | bytes 131072

commit v3 on v2

--- a/solution.py
+++ b/solution.py
@@ -129,8 +129,8 @@
 
     rg = {}
 
-    def forward(s, i):
-        for kind in (1, 0):
+    def forward(s, i, kinds=(0, 1)):
+        for kind in kinds:
             for d in (0, 1):
                 if s > 1:
                     rg[kind, d, s - 1, i].wait_recv()
@@ -383,7 +383,7 @@
             dma((8,)), dma((8,)),
         ],
         compiler_params=pltpu.CompilerParams(
-            collective_id=0, has_side_effects=True, vmem_limit_bytes=60 * 1024 * 1024
+            collective_id=0, has_side_effects=True, vmem_limit_bytes=55040 * 1024
         ),
         cost_estimate=pl.CostEstimate(flops=2_500_000_000, bytes_accessed=4_000_000, transcendentals=0),
     )(orbitals, targets, coulomb)

time: 62.5 us -> 61.4 us (0.982)
  Pallas kernels: 60.5 us -> 59.2 us
    pallas_call x1, Pallas kernels: 60.5 us -> 59.2 us  [body(): pl.pallas_call(kernel, out_shape=jax.ShapeDtypeStruct((16, NB), F32), in_...]
    unnamed x1 -> x3, local copies, waits for them, and re-layouts: 1.47 us -> 1.39 us
where the time goes in v3:
time: 61.4 us; the launch traced here: 60.6 us
  Pallas kernels  59.2 us (96%)
  local copies, waits for them, and re-layouts  1.39 us (2%)
    pallas_call x1, Pallas kernels, body(): pl.pallas_call(kernel, out_shape=jax.ShapeDtypeStruct((16, NB), F32), in_...  59.2 us
    unnamed x3, local copies, waits for them, and re-layouts  1.39 us

profile of v3, /device:TPU:1, one launch (start us, length us, event | category | flops | bytes accessed | tf_op | source)
XLA Modules:
  0.0 60.6 jit_solution(1775498672451387853)
XLA Ops:
  0.0 0.0 copy-start
  0.0 0.8 %copy-done = bf16[16,1024]{1,0:T(8,128)(2,1)S(1)} copy-done((bf16[16,1024]{1,0:T(8,128)(2,1)S(1)}, bf16[16,1024]{1,0:T(8,128)(2,1)}, u32[]{:S(2)}) %copy-start) | copy-done | bytes 32792
  0.8 59.2 %shard_map.37 = f32[16,1024]{1,0:T(8,128)S(1)} custom-call(bf16[16,8192]{1,0:T(8,128)(2,1)} %orb.1, bf16[16,1024]{1,0:T(8,128)(2,1)S(1)} %copy-done, f32[512,256]{1,0:T(8,128)} %cou.1), custom_call_target="tpu_custom_call" | custom-call | flops 2500000000 | bytes 4000000 | tf_op jit(solution)/shard_map/pallas_call | solution.py:349
  59.9 0.6 %copy.5 = f32[16,1024]{1,0:T(8,128)} copy(f32[16,1024]{1,0:T(8,128)S(1)} %shard_map.37) | data formatting | bytes 131072
Async XLA Ops:
  0.0 0.8 %copy-start = (bf16[16,1024]{1,0:T(8,128)(2,1)S(1)}, bf16[16,1024]{1,0:T(8,128)(2,1)}, u32[]{:S(2)}) copy-start(bf16[16,1024]{1,0:T(8,128)(2,1)} %tgt.1) | copy-start | bytes 98308

commit v4 on v3

--- a/solution.py
+++ b/solution.py
@@ -22,6 +22,7 @@
     ((slice(1, 6), slice(768, 896)), (slice(1, 6), slice(896, 1024))),
 )
 DX = (0, 1, 3, 2)
+ORDER = ((0, 1, 2, 3), (0, 2, 3, 1))
 
 
 def kernel(
@@ -132,19 +133,20 @@
     def forward(s, i, kinds=(0, 1)):
         for kind in kinds:
             for d in (0, 1):
+                j = ORDER[d][i]
                 if s > 1:
-                    rg[kind, d, s - 1, i].wait_recv()
-                if s < 4 or (d == 0) == (i < 2):
-                    rg[kind, d, s, i] = go(ring(kind, d, s, i))
+                    rg[kind, d, s - 1, j].wait_recv()
+                if s < 4 or (d == 0) == (j < 2):
+                    rg[kind, d, s, j] = go(ring(kind, d, s, j))
 
     b_own = []
     for i, dx in enumerate(DX):
         if dx == 0:
             a_in.wait()
             swaps[0, 1].wait_recv()
-        else:
-            swaps[dx, 0].wait_recv()
-            swaps[dx, 1].wait_recv()
+        for near in ((), (1, 3), (2,), ())[i]:
+            swaps[near, 0].wait_recv()
+            swaps[near, 1].wait_recv()
         forward(1, i)
         cp = pltpu.make_async_copy(A.at[1, chunk[i]], B.at[1, chunk[i]], loc.at[3 + i])
         cp.start()

time: 61.4 us -> 61.3 us (level)
  no operation moved by 1% of the time
where the time goes in v4:
time: 61.3 us; the launch traced here: 60.7 us
  Pallas kernels  59.3 us (97%)
  local copies, waits for them, and re-layouts  1.39 us (2%)
    pallas_call x1, Pallas kernels, body(): pl.pallas_call(kernel, out_shape=jax.ShapeDtypeStruct((16, NB), F32), in_...  59.3 us
    unnamed x3, local copies, waits for them, and re-layouts  1.39 us

profile of v4, /device:TPU:1, one launch (start us, length us, event | category | flops | bytes accessed | tf_op | source)
XLA Modules:
  0.0 60.7 jit_solution(11293498997278255048)
XLA Ops:
  0.0 0.0 copy-start
  0.0 0.8 %copy-done = bf16[16,1024]{1,0:T(8,128)(2,1)S(1)} copy-done((bf16[16,1024]{1,0:T(8,128)(2,1)S(1)}, bf16[16,1024]{1,0:T(8,128)(2,1)}, u32[]{:S(2)}) %copy-start) | copy-done | bytes 32792
  0.8 59.3 %shard_map.37 = f32[16,1024]{1,0:T(8,128)S(1)} custom-call(bf16[16,8192]{1,0:T(8,128)(2,1)} %orb.1, bf16[16,1024]{1,0:T(8,128)(2,1)S(1)} %copy-done, f32[512,256]{1,0:T(8,128)} %cou.1), custom_call_target="tpu_custom_call" | custom-call | flops 2500000000 | bytes 4000000 | tf_op jit(solution)/shard_map/pallas_call | solution.py:351
  60.1 0.6 %copy.5 = f32[16,1024]{1,0:T(8,128)} copy(f32[16,1024]{1,0:T(8,128)S(1)} %shard_map.37) | data formatting | bytes 131072
Async XLA Ops:
  0.0 0.8 %copy-start = (bf16[16,1024]{1,0:T(8,128)(2,1)S(1)}, bf16[16,1024]{1,0:T(8,128)(2,1)}, u32[]{:S(2)}) copy-start(bf16[16,1024]{1,0:T(8,128)(2,1)} %tgt.1) | copy-start | bytes 98308

commit v5 on v4

--- a/solution.py
+++ b/solution.py
@@ -313,33 +313,36 @@
     for k in range(4):
         td[k].wait_recv()
 
-    left = S[...].reshape(128, 1024)
-    for q in range(4):
-        cols = slice(q * 256, (q + 1) * 256)
-        part = jnp.dot(left, T[:, :, :, :, cols].reshape(1024, 256), preferred_element_type=F32)
-        part = part.reshape(8, 16, 256)
-        for k in range(3):
-            OO[k, :, cols] = part[SLOT[(0, 2, -2)[k]]]
-        OB[:, :, cols] = part.astype(BF16)
-
     def o_send(n, src, dst, dz):
         return go(remote(src, dst, o_s.at[n], o_r.at[n], at(dz=dz)))
 
-    far = [o_send(d, OB.at[0, :, half[d]], OH.at[d], 2 - 4 * d) for d in (0, 1)]
-    far += [o_send(2 + d, OB.at[SLOT[3 - 6 * d]], OA.at[d], 1 - 2 * d) for d in (0, 1)]
-    near = [o_send(4 + d, OB.at[SLOT[1 - 2 * d]], OR.at[d], 1 - 2 * d) for d in (0, 1)]
-    for d in (0, 1):
-        far[d].wait_recv()
-        far[2 + d].wait_recv()
-        for h in (0, 1):
+    left = S[...].reshape(128, 1024)
+    far, third, near = {}, {}, []
+    for h in (0, 1):
+        for q in (2 * h, 2 * h + 1):
+            cols = slice(q * 256, (q + 1) * 256)
+            part = jnp.dot(left, T[:, :, :, :, cols].reshape(1024, 256), preferred_element_type=F32)
+            part = part.reshape(8, 16, 256)
+            for k in range(3):
+                OO[k, :, cols] = part[SLOT[(0, 2, -2)[k]]]
+            OB[:, :, cols] = part.astype(BF16)
+        far[h] = o_send(h, OB.at[0, :, half[h]], OH.at[h], 2 - 4 * h)
+        for d in (0, 1):
+            third[h, d] = o_send(2 + 2 * h + d, OB.at[SLOT[3 - 6 * d], :, half[h]], OA.at[d, :, half[h]], 1 - 2 * d)
+    near = [o_send(6 + d, OB.at[SLOT[1 - 2 * d]], OR.at[d], 1 - 2 * d) for d in (0, 1)]
+    for h in (0, 1):
+        far[h].wait_recv()
+        for d in (0, 1):
+            third[h, d].wait_recv()
             joined = OO[1 + d, :, half[h]] + OA[d, :, half[h]].astype(F32)
             if h == d:
                 joined = joined + OH[d].astype(F32)
             OC[d, :, half[h]] = joined.astype(BF16)
-        near.append(o_send(6 + d, OC.at[d], OR.at[2 + d], 2 - 4 * d))
+            near.append(o_send(8 + 2 * h + d, OC.at[d, :, half[h]], OR.at[2 + d, :, half[h]], 2 - 4 * d))
+    for cp in near:
+        cp.wait_recv()
     total = OO[0]
     for n in range(4):
-        near[n].wait_recv()
         total = total + OR[n].astype(F32)
     out[...] = total
     for cp in started:
@@ -382,7 +385,7 @@
             dma((3,)), dma((3,)),
             dma((5,)), dma((5,)),
             dma((20,)), dma((20,)),
-            dma((8,)), dma((8,)),
+            dma((12,)), dma((12,)),
         ],
         compiler_params=pltpu.CompilerParams(
             collective_id=0, has_side_effects=True, vmem_limit_bytes=55040 * 1024

time: 61.3 us -> 61.3 us (level)
  no operation moved by 1% of the time
where the time goes in v5:
time: 61.3 us; the launch traced here: 60.6 us
  Pallas kernels  59.2 us (97%)
  local copies, waits for them, and re-layouts  1.39 us (2%)
    pallas_call x1, Pallas kernels, body(): pl.pallas_call(kernel, out_shape=jax.ShapeDtypeStruct((16, NB), F32), in_...  59.2 us
    unnamed x3, local copies, waits for them, and re-layouts  1.39 us

profile of v5, /device:TPU:1, one launch (start us, length us, event | category | flops | bytes accessed | tf_op | source)
XLA Modules:
  0.0 60.6 jit_solution(16084869333610492687)
XLA Ops:
  0.0 0.0 copy-start
  0.0 0.8 %copy-done = bf16[16,1024]{1,0:T(8,128)(2,1)S(1)} copy-done((bf16[16,1024]{1,0:T(8,128)(2,1)S(1)}, bf16[16,1024]{1,0:T(8,128)(2,1)}, u32[]{:S(2)}) %copy-start) | copy-done | bytes 32792
  0.8 59.2 %shard_map.37 = f32[16,1024]{1,0:T(8,128)S(1)} custom-call(bf16[16,8192]{1,0:T(8,128)(2,1)} %orb.1, bf16[16,1024]{1,0:T(8,128)(2,1)S(1)} %copy-done, f32[512,256]{1,0:T(8,128)} %cou.1), custom_call_target="tpu_custom_call" | custom-call | flops 2500000000 | bytes 4000000 | tf_op jit(solution)/shard_map/pallas_call | solution.py:354
  59.9 0.6 %copy.5 = f32[16,1024]{1,0:T(8,128)} copy(f32[16,1024]{1,0:T(8,128)S(1)} %shard_map.37) | data formatting | bytes 131072
Async XLA Ops:
  0.0 0.8 %copy-start = (bf16[16,1024]{1,0:T(8,128)(2,1)S(1)}, bf16[16,1024]{1,0:T(8,128)(2,1)}, u32[]{:S(2)}) copy-start(bf16[16,1024]{1,0:T(8,128)(2,1)} %tgt.1) | copy-start | bytes 98308
